TPU v7x, 32 devices: a whole 2x2x4 slice. The times are simulated.
32 devices in a mesh: segment: 4 (over y, x), blk: 8 (over z, core).
Axes of the slice: x: 2, y: 2, z: 4, core: 2. Of those that a mesh axis runs over, the one named last changes fastest.
Arguments:
- echoes: bfloat16 [4, 512, 128, 512], P('segment', 'blk'), may hold values from -6 to 6
- train_blocks: int32 [4, 256, 6], P('segment', 'blk'), may hold values from 0 to 15, as said below
- hard_bins: int32 [4, 256], P('segment', 'blk'), may hold values 0 or 1
- owner_map: int32 [256], replicated, may hold values from 0 to 255, each once
- code_phase: float32 [64], replicated, may hold values from -3.140625 to 3.140625
Outputs:
- returns: bfloat16 [4, 256, 512, 256], P('segment', 'blk')
Inputs may be any that keep to these rules, and one draw needn't show every extreme that they name: `train_blocks`: each row lists 6 different training blocks.
All inputs are finite; a program needn't handle non-finite values. No bound on the sum of `hard_bins` on one device may be relied on, other than what follows from the above.
Results may differ from a plain program's by a relative error of at most 0.0086.
Values may be sent and summed in bfloat16 or wider, within the bound.
A program may use at most 128 MiB of HBM per device.

v0:
```python
import math

import jax
import jax.numpy as jnp
from jax import lax
from jax.sharding import PartitionSpec as P

CH = 128
BEAMS = 128
RB = 32
NTR_EASY = 3
NS_STEPS = 12
CBLK = 128


decay_rate = 0.7
diag_load = 0.1
highest = lax.Precision.HIGHEST


def entering(value, axis, join, neutral):
    count, mine = (lax.axis_size(axis), lax.axis_index(axis))
    pieces = jax.tree.map(lambda part: lax.all_gather(part, axis), value)
    total = jax.tree.map(
        lambda part, zero: jnp.full_like(part, 0) + jnp.asarray(zero, part.dtype), value, neutral
    )

    def turn(position, total):
        longer = join(total, jax.tree.map(lambda part: part[position], pieces))
        return jax.tree.map(lambda new, old: jnp.where(position < mine, new, old), longer, total)

    return lax.fori_loop(0, count - 1, turn, total)


def doppler_table(owner_map, pulse_count):
    pulse_index = jnp.arange(pulse_count, dtype=jnp.int32)
    phase_steps = pulse_index[:, None] * owner_map[None, :] % pulse_count
    angles = phase_steps.astype(jnp.float32) * (2.0 * math.pi / pulse_count)
    cosine = jnp.cos(angles) / math.sqrt(pulse_count)
    sine_part = jnp.sin(angles) / math.sqrt(pulse_count)
    real_rows = jnp.stack([cosine, -sine_part], axis=1)
    imag_rows = jnp.stack([sine_part, cosine], axis=1)
    return jnp.concatenate([real_rows, imag_rows], axis=0).astype(jnp.bfloat16)


def covariance_half(spectra, blocks, hard, block_len, easy_count):
    bin_count, range_count, row_width = spectra.shape
    channels = row_width // 2
    listed = blocks.shape[1]
    blocked = spectra.reshape(bin_count, range_count // block_len, block_len, row_width)
    chosen = jnp.take_along_axis(blocked, blocks[:, :, None, None], axis=1)
    keep_mask = (jnp.arange(listed, dtype=jnp.int32)[None, :] < easy_count) | (hard[:, None] == 1)
    weighted = chosen * keep_mask[:, :, None, None].astype(jnp.bfloat16)
    train_rows = chosen.reshape(bin_count, listed * block_len, row_width)
    weighted = weighted.reshape(bin_count, listed * block_len, row_width)
    real_part = train_rows[..., :channels]
    imag_part = train_rows[..., channels:]
    left_side = jnp.concatenate(
        [train_rows, jnp.concatenate([imag_part, -real_part], axis=-1)], axis=1
    )
    right_side = jnp.concatenate([weighted[..., :channels], weighted[..., channels:]], axis=1)
    gram_sum = jnp.einsum("nsf,nsg->nfg", left_side, right_side, preferred_element_type=jnp.float32)
    row_count = jnp.where(hard == 1, listed * block_len, easy_count * block_len).astype(jnp.float32)
    return gram_sum / row_count[:, None, None]


def steering(channels, beams):
    channel_index = jnp.arange(channels, dtype=jnp.int32)
    beam_index = jnp.arange(beams, dtype=jnp.int32)
    phase_steps = channel_index[:, None] * (2 * beam_index[None, :] - beams) % (2 * beams)
    angles = phase_steps.astype(jnp.float32) * (math.pi / beams)
    return (jnp.cos(angles) / math.sqrt(channels), jnp.sin(angles) / math.sqrt(channels))


def complex_product(first_re, first_im, second_re, second_im):

    def matmul(first, second):
        return jnp.einsum("nij,njk->nik", first, second, precision=highest)

    return (
        matmul(first_re, second_re) - matmul(first_im, second_im),
        matmul(first_re, second_im) + matmul(first_im, second_re),
    )


def beam_weights(cov_half, steer_re, steer_im, steps):
    channels = cov_half.shape[2]
    identity = jnp.eye(channels, dtype=jnp.float32)
    cov_re = cov_half[:, :channels] + diag_load * identity
    cov_im = cov_half[:, channels:]
    trace_value = jnp.trace(cov_re, axis1=1, axis2=2)
    start_re = identity[None] / trace_value[:, None, None]
    start_im = jnp.zeros_like(start_re)

    def newton(step_index, inverse_pair):
        inverse_re, inverse_im = inverse_pair
        middle_re, middle_im = complex_product(cov_re, cov_im, inverse_re, inverse_im)
        return complex_product(inverse_re, inverse_im, 2.0 * identity - middle_re, -middle_im)

    inverse_re, inverse_im = lax.fori_loop(0, steps, newton, (start_re, start_im))

    def apply(matrix, table):
        return jnp.einsum("nij,jb->nib", matrix, table, precision=highest)

    vec_re = apply(inverse_re, steer_re) - apply(inverse_im, steer_im)
    vec_im = apply(inverse_re, steer_im) + apply(inverse_im, steer_re)
    beam_gain = jnp.sum(steer_re * vec_re + steer_im * vec_im, axis=1)
    weight_re = vec_re / beam_gain[:, None, :]
    weight_im = vec_im / beam_gain[:, None, :]
    upper_rows = jnp.concatenate([weight_re, -weight_im], axis=2)
    lower_rows = jnp.concatenate([weight_im, weight_re], axis=2)
    return jnp.concatenate([upper_rows, lower_rows], axis=1).astype(jnp.bfloat16)


def compression_table(code_phase, block_len):
    length = code_phase.shape[0]
    input_pos = jnp.arange(2 * block_len, dtype=jnp.int32)[:, None]
    output_pos = jnp.arange(block_len, dtype=jnp.int32)[None, :]
    lag_index = input_pos - output_pos
    onehot = (lag_index[:, :, None] == jnp.arange(length, dtype=jnp.int32)[None, None, :]).astype(
        jnp.float32
    )
    code_table = jnp.stack([jnp.cos(code_phase), jnp.sin(code_phase)]) / math.sqrt(length)
    table = jnp.einsum("qpl,kl->qkp", onehot, code_table, precision=highest)
    return table.astype(jnp.bfloat16)


def compress(formed, table, block_len):
    bin_count, range_count, row_width = formed.shape
    beam_half = row_width // 2
    blocks = formed.reshape(bin_count, range_count // block_len, block_len, row_width)
    next_blocks = jnp.concatenate([blocks[:, 1:], jnp.zeros_like(blocks[:, :1])], axis=1)
    paired = jnp.concatenate([blocks, next_blocks], axis=2)
    mixed_terms = jnp.einsum("nbqe,qkp->nbkpe", paired, table, preferred_element_type=jnp.float32)
    result_re = mixed_terms[:, :, 0, :, :beam_half] + mixed_terms[:, :, 1, :, beam_half:]
    result_im = mixed_terms[:, :, 0, :, beam_half:] - mixed_terms[:, :, 1, :, :beam_half]
    joined = jnp.concatenate([result_re, result_im], axis=-1)
    return joined.reshape(bin_count, range_count, row_width).astype(jnp.bfloat16)


def local(echoes, train_blocks, hard_bins, owner_map, code_phase):
    samples = echoes[0]
    range_local, channels, double_pulses = samples.shape
    dft_table = doppler_table(owner_map, double_pulses // 2)
    spectra = jnp.einsum("rcp,pkj->jrkc", samples, dft_table, preferred_element_type=jnp.float32)
    spectra = spectra.astype(jnp.bfloat16).reshape(dft_table.shape[2], range_local, 2 * channels)
    owned = lax.all_to_all(spectra, "blk", split_axis=0, concat_axis=1, tiled=True)
    partial_cov = covariance_half(owned, train_blocks[0], hard_bins[0], RB, NTR_EASY)

    def combine(earlier, later):
        return (earlier[0] * later[0], later[0] * earlier[1] + later[1])

    factor_scan, carried = entering(
        (jnp.full((), decay_rate, jnp.float32), partial_cov),
        "segment",
        combine,
        (jnp.ones((), jnp.float32), jnp.zeros_like(partial_cov)),
    )
    steer_re, steer_im = steering(CH, BEAMS)
    weights = beam_weights(carried, steer_re, steer_im, NS_STEPS)
    formed = jnp.einsum("nrf,nfe->nre", owned, weights, preferred_element_type=jnp.float32).astype(
        jnp.bfloat16
    )
    comp_table = compression_table(code_phase, CBLK)
    return compress(formed, comp_table, CBLK)[None]


def solution(mesh):
    in_specs = (
        P("segment", "blk", None, None),
        P("segment", "blk", None),
        P("segment", "blk"),
        P(),
        P(),
    )
    out_specs = P("segment", "blk", None, None)
    return jax.shard_map(local, mesh=mesh, in_specs=in_specs, out_specs=out_specs, check_vma=False)
```

profile of v0, /device:TPU:0, one launch (start us, length us, event | category | flops | bytes accessed | tf_op | source)
XLA Modules:
  0.0 956.5 jit_solution(788133831316558868)
XLA Ops:
  8.4 10.1 %convert_bitcast_fusion = bf16[256,64,2,128]{0,3,1,2:T(8,128)(2,1)} fusion(bf16[1,64,128,512]{3,2,1,0:T(8,128)(2,1)} %param.9, bf16[256,1,256]{2,0,1:T(8,128)(2,1)S(1)} %get-tuple-element.226, bf16[256,1,256]{2,0,1:T(8,128)(2,1)S(1)} %get-tuple-element.225, bf16[256,1,256]{2,0,1:T(8,128)(2,1)S(1)} %get-tuple-element.224), kind=kOutput, calls=%fused_computation.26 | convolution fusion | flops 4301258752 | bytes 17170432 | tf_op jit(solution)/shard_map/rcp,pkj->jrkc/dot_general | solution.py:145
  18.5 7.7 copy.118
  26.2 12.1 %copy.119 = bf16[256,64,256]{2,1,0:T(8,128)(2,1)} copy(bf16[256,64,256]{0,2,1:T(8,128)(2,1)} %bitcast.137) | data formatting | bytes 16777216 | tf_op jit(solution)/shard_map/reshape | solution.py:146
  38.3 6.5 all-to-all-start
  45.8 183.0 %all-to-all-done = bf16[256,64,256]{2,1,0:T(8,128)(2,1)} async-done(((bf16[256,64,256]{2,1,0:T(8,128)(2,1)}), bf16[256,64,256]{2,1,0:T(8,128)(2,1)}, u32[]{:S(2)}, u32[]{:S(2)}) %all-to-all-start) | async-done | bytes 8388640 | tf_op jit(solution)/shard_map/all_to_all | solution.py:147
  228.8 8.4 copy.120
  251.3 10.3 %all-reduce.1 = f32[4]{0:T(128)S(1)} all-reduce(f32[4]{0:T(128)S(1)} %dynamic-update-slice), channel_id=1, replica_groups=mesh['segment'=4,'blk'=8] {'segment'}, use_global_device_ids=true, to_apply=%add.1 | all-reduce | flops 4 | bytes 32
  264.8 140.9 %all-gather.3.cloned.1.call-done = f32[128,256,128]{2,1,0:T(8,128)} async-done(((f32[32,256,128]{2,1,0:T(8,128)}), f32[128,256,128]{2,1,0:T(8,128)}) %all-gather.3.cloned.1.call-update) | async-done | bytes 16777232 | tf_op jit(solution)/shard_map/all_gather | solution.py:23
  405.7 21.7 %while.28 = (s32[]{:T(128)}, f32[32,256,128]{2,1,0:T(8,128)}, s32[]{:T(128)}, f32[4]{0:T(128)S(1)}, f32[4,32,256,128]{3,2,1,0:T(8,128)}, /*index=5*/s32[]{:T(128)}, s32[]{:T(128)}) while((s32[]{:T(128)}, f32[32,256,128]{2,1,0:T(8,128)}, s32[]{:T(128)}, f32[4]{0:T(128)S(1)}, f32[4,32,256,128]{3,2,1,0:T(8,128)}, ...), condition=%wide.region_1.2_spmd.clone, body=%wide.region_0.1_spmd.clone.sunk | while | flops 4194308 | bytes 12583037 | solution.py:32
  406.3 5.8 fusion.177
  412.7 7.1 fusion.177
  420.3 7.1 fusion.177
  433.7 453.6 %while.27 = (s32[]{:T(128)}, f32[32,128,128]{1,2,0:T(8,128)S(1)}, f32[32,128,128]{1,2,0:T(8,128)}, f32[32,128,128]{2,1,0:T(8,128)}, f32[32,128,128]{2,1,0:T(8,128)}, /*index=5*/s32[]{:T(128)}) while((s32[]{:T(128)}, f32[32,128,128]{1,2,0:T(8,128)S(1)}, f32[32,128,128]{1,2,0:T(8,128)}, f32[32,128,128]{2,1,0:T(8,128)}, ...), condition=%wide.region_4.5_spmd.clone, body=%wide.region_3.4_spmd.clone.sunk | while | flops 6445629440 | bytes 79822968 | solution.py:100
  482.3 5.0 add_bitcast_fusion.2
  518.6 5.0 add_bitcast_fusion.2
  554.9 5.0 add_bitcast_fusion.2
  772.9 5.0 add_bitcast_fusion.2
  809.2 5.0 add_bitcast_fusion.2
  845.6 5.0 add_bitcast_fusion.2
  881.9 5.0 add_bitcast_fusion.2
  898.7 10.5 %convolution_convert_fusion = bf16[32,512,256]{2,1,0:T(8,128)(2,1)} fusion(bf16[32,512,256]{2,1,0:T(8,128)(2,1)} %bitcast.142, bf16[32,128,128]{1,2,0:T(8,128)(2,1)S(1)} %get-tuple-element.223, bf16[32,128,128]{1,2,0:T(8,128)(2,1)S(1)} %get-tuple-element.222, bf16[32,128,128]{1,2,0:T(8,128)(2,1)S(1)} %get-tuple-element.221), kind=kOutput, calls=%fused_computation.29 | convolution fusion | flops 2168455168 | bytes 19922944 | tf_op jit(solution)/shard_map/nrf,nfe->nre/dot_general | solution.py:161
  912.8 15.3 %convolution_bitcast_fusion = f32[32,4,2,128,256]{4,3,1,0,2:T(8,128)} fusion(bf16[32,3,128,256]{3,2,1,0:T(8,128)(2,1)S(1)} %slice.50, bf16[32,4,128,256]{3,2,1,0:T(8,128)(2,1)} %bitcast.145, bf16[256,2,128,1,1]{2,1,0,4,3:T(2,128)(2,1)S(1)} %fusion.37), kind=kOutput, calls=%fused_computation.12 | convolution fusion | flops 4345298944 | bytes 48365568 | tf_op jit(solution)/shard_map/nbqe,qkp->nbkpe/dot_general | solution.py:134
  928.1 14.8 %fusion.12 = (bf16[32,4,1,128,128]{4,3,1,0,2:T(8,128)(2,1)S(1)}, bf16[32,4,1,128,128]{4,3,1,0,2:T(8,128)(2,1)}) fusion(f32[32,4,2,128,256]{4,3,1,0,2:T(8,128)} %convolution_bitcast_fusion), kind=kLoop, calls=%fused_computation.21 | loop fusion | flops 8388608 | bytes 41943040 | tf_op jit(solution)/shard_map/convert.3
  942.9 6.5 pad_maximum_fusion
  (217 shorter events, 443.1 us)
Async XLA Ops:
  38.3 6.5 copy-start.3
  38.3 6.6 copy-start.4
  38.3 190.5 %all-to-all-start = ((bf16[256,64,256]{2,1,0:T(8,128)(2,1)}), bf16[256,64,256]{2,1,0:T(8,128)(2,1)}, u32[]{:S(2)}, u32[]{:S(2)}) async-start(bf16[256,64,256]{2,1,0:T(8,128)(2,1)} %copy.119), calls=%async_computation | async-start | bytes 16777216 | tf_op jit(solution)/shard_map/all_to_all | solution.py:147
  44.8 360.9 %all-gather.3.cloned.1.call-start = ((), (), s32[]{:S(2)}) async-start(), calls=%async_computation.1 | async-start | bytes 20971520 | tf_op jit(solution)/shard_map/all_gather | solution.py:23
  249.2 12.5 %copy-start.5 = (f32[64]{0:T(128)S(1)}, f32[64]{0:T(128)}, u32[]{:S(2)}) copy-start(f32[64]{0:T(128)} %param.13) | copy-start | bytes 772
  451.0 2.2 copy-start
  453.2 4.5 copy-start.1
  487.3 2.2 copy-start
  489.5 4.5 copy-start.1
  523.6 2.2 copy-start
  525.8 4.5 copy-start.1
  562.2 4.5 copy-start.1
  596.3 2.2 copy-start
  598.5 4.5 copy-start.1
  632.6 2.2 copy-start
  634.8 4.5 copy-start.1
  668.9 2.2 copy-start
  671.2 4.5 copy-start.1
  707.5 4.5 copy-start.1
  743.8 4.5 copy-start.1
  780.1 4.5 copy-start.1
  816.5 4.5 copy-start.1
  852.8 4.5 copy-start.1
  889.7 2.4 copy-start.2
  (7 other events, 14.0 us)
Sparse Core Ops, SparseCore 0:
  249.3 156.3 all-gather.2
where the time goes:
time: 964 us; the launch traced here: 956 us
  matrix products  462 us (48%)
  waiting for transfers between devices  324 us (34%)
  local copies, waits for them, and re-layouts  69.6 us (7%)
  other arithmetic  52.3 us (5%)
  loops' own time  18.4 us (2%)
  between operations  13.8 us (1%)
  blocking collectives  10.3 us (1%)
    dot_general x96, matrix products, matmul(): return jnp.einsum('nij,njk->nik', first, second, precision=highest)  409 us
    all_to_all x1, waiting for transfers between devices, local(): lax.all_to_all(spectra, 'blk', split_axis=0, concat_axis=1, tiled=True)  183 us
    all_gather x1, waiting for transfers between devices, entering(): pieces = jax.tree.map(lambda part: lax.all_gather(part, axis), value)  141 us
    while x60, local copies, waits for them, and re-layouts  26.5 us
    select_n x3, other arithmetic, turn(): jnp.where(position < mine, new, old)  19.9 us
  transfers between devices with their start and end apart: 2, of which 2 were waited for; matrix products, arithmetic and copies ran while one was open for 1% of the time, Pallas kernels for 0%

commit v1 on v0

v1 whole, which is shorter than its diff:
```python
import functools
import math

import jax
import jax.numpy as jnp
from jax import lax
from jax.experimental import pallas as pl
from jax.experimental.pallas import tpu as pltpu
from jax.sharding import PartitionSpec as P

CH = 128
BEAMS = 128
RB = 32
NTR_EASY = 3
NS_STEPS = 12
CBLK = 128
CHUNKS = 4
GROUP = 4

decay_rate = 0.7
diag_load = 0.1
highest = lax.Precision.HIGHEST
f32 = jnp.float32
bf16 = jnp.bfloat16


def doppler_rows(owner_map, pulse_count):
    pulse_index = jnp.arange(pulse_count, dtype=jnp.int32)
    phase_steps = owner_map[:, None] * pulse_index[None, :] % pulse_count
    angles = phase_steps.astype(f32) * (2.0 * math.pi / pulse_count)
    cosine = jnp.cos(angles) / math.sqrt(pulse_count)
    sine_part = jnp.sin(angles) / math.sqrt(pulse_count)
    real_rows = jnp.concatenate([cosine, sine_part], axis=1)
    imag_rows = jnp.concatenate([-sine_part, cosine], axis=1)
    return jnp.stack([real_rows, imag_rows]).astype(bf16)


def steering(channels, beams):
    channel_index = jnp.arange(channels, dtype=jnp.int32)
    beam_index = jnp.arange(beams, dtype=jnp.int32)
    phase_steps = channel_index[:, None] * (2 * beam_index[None, :] - beams) % (2 * beams)
    angles = phase_steps.astype(f32) * (math.pi / beams)
    return (jnp.cos(angles) / math.sqrt(channels), jnp.sin(angles) / math.sqrt(channels))


def compression_rows(code_phase, block_len):
    length = code_phase.shape[0]
    input_pos = jnp.arange(2 * block_len, dtype=jnp.int32)[None, :]
    output_pos = jnp.arange(block_len, dtype=jnp.int32)[:, None]
    lag_index = input_pos - output_pos
    onehot = (lag_index[:, :, None] == jnp.arange(length, dtype=jnp.int32)[None, None, :]).astype(f32)
    code_table = jnp.stack([jnp.cos(code_phase), jnp.sin(code_phase)]) / math.sqrt(length)
    table = jnp.einsum("pql,kl->kpq", onehot, code_table, precision=highest)
    return table.reshape(2 * block_len, 2 * block_len).astype(bf16)


def doppler_kernel(x_ref, t_ref, o_ref, scr):
    rows, channels, _ = x_ref.shape
    slots = o_ref.shape[0]
    pair = 2
    for base in range(0, rows, pair):
        block = x_ref[base : base + pair].reshape(pair * channels, x_ref.shape[2])
        y = lax.dot_general(
            t_ref[...], block, (((1,), (1,)), ((), ())), preferred_element_type=f32
        )
        for i in range(pair):
            part = y[:, i * channels : (i + 1) * channels]
            scr[0, pl.ds(base + i, slots, stride=rows), :] = part[:slots]
            scr[1, pl.ds(base + i, slots, stride=rows), :] = part[slots:]
    for k in range(2):
        o_ref[:, :, k * channels : (k + 1) * channels] = (
            scr[k].reshape(slots, rows, channels).astype(bf16)
        )


def doppler(samples, table):
    ranges, channels, width = samples.shape
    slots = table.shape[0] // 2
    rows = 16
    return pl.pallas_call(
        doppler_kernel,
        grid=(ranges // rows,),
        in_specs=[
            pl.BlockSpec((rows, channels, width), lambda i: (i, 0, 0)),
            pl.BlockSpec(table.shape, lambda i: (0, 0)),
        ],
        out_specs=pl.BlockSpec((slots, rows, 2 * channels), lambda i: (0, i, 0)),
        out_shape=jax.ShapeDtypeStruct((slots, ranges, 2 * channels), bf16),
        scratch_shapes=[pltpu.VMEM((2, slots * rows, channels), f32)],
        compiler_params=pltpu.CompilerParams(vmem_limit_bytes=40 * 2**20),
        cost_estimate=pl.CostEstimate(
            flops=4 * ranges * channels * width * slots,
            bytes_accessed=2 * samples.size + 4 * slots * ranges * channels,
            transcendentals=0,
        ),
    )(samples, table)


def covariance_kernel(m_ref, s_ref, y_ref, o_ref):
    sources, group, rows, width = y_ref.shape
    ch = width // 2
    per = rows // RB
    first = pl.program_id(0) * group
    row = lax.broadcasted_iota(jnp.int32, (ch, ch), 0)
    col = lax.broadcasted_iota(jnp.int32, (ch, ch), 1)
    for g in range(group):
        y = y_ref[:, g].reshape(sources * rows, width)
        parts = []
        for b in range(sources * per):
            keep = m_ref[first + g, b]
            parts.append((y[b * RB : (b + 1) * RB].astype(f32) * keep).astype(bf16))
        masked = jnp.concatenate(parts, axis=0)
        gram = lax.dot_general(
            masked, y, (((0,), (0,)), ((), ())), preferred_element_type=f32
        )
        re = gram[:ch, :ch] + gram[ch:, ch:]
        im = gram[ch:, :ch] - gram[:ch, ch:]
        o_ref[g] = jnp.where(row <= col, re, im) * s_ref[0, first + g]


def covariance(owned, mask, scale, group):
    sources, bins, rows, width = owned.shape
    ch = width // 2
    return pl.pallas_call(
        covariance_kernel,
        grid=(bins // group,),
        in_specs=[
            pl.BlockSpec(memory_space=pltpu.SMEM),
            pl.BlockSpec(memory_space=pltpu.SMEM),
            pl.BlockSpec((sources, group, rows, width), lambda i: (0, i, 0, 0)),
        ],
        out_specs=pl.BlockSpec((group, ch, ch), lambda i: (i, 0, 0)),
        out_shape=jax.ShapeDtypeStruct((bins, ch, ch), f32),
        compiler_params=pltpu.CompilerParams(vmem_limit_bytes=40 * 2**20),
        cost_estimate=pl.CostEstimate(
            flops=2 * owned.size * width, bytes_accessed=2 * owned.size, transcendentals=0
        ),
    )(mask, scale, owned)


def split(x):
    hi = x.astype(bf16)
    return hi, (x - hi.astype(f32)).astype(bf16)


def full(half):
    ch = half.shape[1]
    re, im = half[:ch], half[ch:]
    return jnp.concatenate(
        [jnp.concatenate([re, -im], axis=1), jnp.concatenate([im, re], axis=1)], axis=0
    )


def left(half):
    hi, lo = split(half)
    return jnp.concatenate([full(hi), full(lo)], axis=0)


def right(half):
    return jnp.concatenate(split(half), axis=1)


def product(left_pair, right_pair):
    n = left_pair.shape[0] // 2
    ch = right_pair.shape[1] // 2
    p = jnp.dot(left_pair, right_pair, preferred_element_type=f32)
    return p[:n, :ch] + (p[:n, ch:] + p[n:, :ch])


def beam_kernel(terms, steps, *refs):
    cov_refs = refs[:terms]
    y_ref, sp_ref, st_ref, c_ref = refs[terms : terms + 4]
    o_ref, a_scr, x_scr = refs[-3:]
    sources, group, rows, width = y_ref.shape
    ch = width // 2
    ranges = sources * rows
    row = lax.broadcasted_iota(jnp.int32, (ch, ch), 0)
    col = lax.broadcasted_iota(jnp.int32, (ch, ch), 1)
    eye = (row == col).astype(f32)
    two_eye = jnp.concatenate([2.0 * eye, jnp.zeros_like(eye)], axis=0)
    for g in range(group):
        packed = cov_refs[0][g]
        for d in range(1, terms):
            packed = packed + (decay_rate**d) * cov_refs[d][g]
        flipped = packed.T
        re = jnp.where(row <= col, packed, flipped) + diag_load * eye
        im = jnp.where(row > col, packed, jnp.where(row < col, -flipped, 0.0))
        trace_value = jnp.sum(jnp.sum(re * eye, axis=1, keepdims=True), axis=0, keepdims=True)
        a_scr[g] = left(jnp.concatenate([re, im], axis=0))
        x_scr[g] = jnp.concatenate([eye / trace_value, jnp.zeros_like(eye)], axis=0)

    def newton(step, carry):
        held = [x_scr[g] for g in range(group)]
        middle = [two_eye - product(a_scr[g], right(held[g])) for g in range(group)]
        for g in range(group):
            x_scr[g] = product(left(held[g]), right(middle[g]))
        return carry

    lax.fori_loop(0, steps, newton, 0)
    for g in range(group):
        vec = product(left(x_scr[g]), sp_ref[...])
        gain = jnp.sum(st_ref[...] * vec, axis=0, keepdims=True)
        weights = full((vec / gain).astype(bf16))
        y = y_ref[:, g].reshape(ranges, width)
        formed = jnp.dot(y, weights, preferred_element_type=f32).astype(bf16)
        for base in range(0, ranges, CBLK):
            depth = min(2 * CBLK, ranges - base)
            mixed = jnp.dot(
                c_ref[:, :depth], formed[base : base + depth], preferred_element_type=f32
            )
            out_re = mixed[:CBLK, :ch] + mixed[CBLK:, ch:]
            out_im = mixed[:CBLK, ch:] - mixed[CBLK:, :ch]
            o_ref[g, base : base + CBLK, :] = jnp.concatenate([out_re, out_im], axis=1).astype(bf16)


def beams(covs, owned, steer_pair, steer, comp, earlier, chunk, total_bins, group):
    sources, bins, rows, width = owned.shape
    ch = width // 2
    ranges = sources * rows
    steps = bins // group
    offset = chunk * steps
    in_specs = [pl.BlockSpec((group, ch, ch), lambda i: (i, 0, 0)) for _ in covs] + [
        pl.BlockSpec((sources, group, rows, width), lambda i: (0, i, 0, 0)),
        pl.BlockSpec(steer_pair.shape, lambda i: (0, 0)),
        pl.BlockSpec(steer.shape, lambda i: (0, 0)),
        pl.BlockSpec(comp.shape, lambda i: (0, 0)),
    ]
    operands = [*covs, owned, steer_pair, steer, comp]
    aliases = {}
    if earlier is not None:
        aliases = {len(operands): 0}
        operands.append(earlier)
        in_specs.append(pl.BlockSpec(memory_space=pl.ANY))
    return pl.pallas_call(
        functools.partial(beam_kernel, len(covs), NS_STEPS),
        grid=(steps,),
        in_specs=in_specs,
        out_specs=pl.BlockSpec((None, group, ranges, width), lambda i: (0, offset + i, 0, 0)),
        out_shape=jax.ShapeDtypeStruct((1, total_bins, ranges, width), bf16),
        scratch_shapes=[
            pltpu.VMEM((group, 4 * ch, 2 * ch), bf16),
            pltpu.VMEM((group, 2 * ch, ch), f32),
        ],
        input_output_aliases=aliases,
        compiler_params=pltpu.CompilerParams(vmem_limit_bytes=48 * 2**20),
        cost_estimate=pl.CostEstimate(
            flops=bins * (2 * NS_STEPS * 2 * 4 * ch * 4 * ch * ch * 2),
            bytes_accessed=4 * owned.size,
            transcendentals=0,
        ),
    )(*operands)


def local(echoes, train_blocks, hard_bins, owner_map, code_phase):
    samples = echoes[0]
    ranges_local, channels, double_pulses = samples.shape
    owners = lax.axis_size("blk")
    segments = lax.axis_size("segment")
    blocks, hard = train_blocks[0], hard_bins[0]
    bins, listed = blocks.shape
    chunks = CHUNKS
    while bins % chunks:
        chunks //= 2
    part = bins // chunks
    group = math.gcd(part, GROUP)

    table = doppler_rows(owner_map, double_pulses // 2).reshape(
        2, owners, chunks, part, double_pulses
    )
    keep = (jnp.arange(listed, dtype=jnp.int32)[None, :] < NTR_EASY) | (hard[:, None] == 1)
    total_blocks = owners * ranges_local // RB
    mask = (
        ((blocks[:, :, None] == jnp.arange(total_blocks, dtype=jnp.int32)) & keep[:, :, None])
        .any(axis=1)
        .astype(f32)
    )
    counted = jnp.where(hard == 1, listed * RB, NTR_EASY * RB).astype(f32)
    scale = 1.0 / counted
    steer = jnp.concatenate(steering(channels, BEAMS), axis=0)
    steer_hi = lax.reduce_precision(steer, 8, 7)
    steer_pair = jnp.concatenate([steer_hi.astype(bf16), (steer - steer_hi).astype(bf16)], axis=1)
    comp = compression_rows(code_phase, CBLK)

    owned, covs = [], []
    for c in range(chunks):
        spectra = doppler(samples, table[:, :, c].reshape(2 * owners * part, double_pulses))
        spectra = spectra.reshape(owners, part, ranges_local, 2 * channels)
        owned.append(lax.all_to_all(spectra, "blk", split_axis=0, concat_axis=0, tiled=True))
    for c in range(chunks):
        span = slice(c * part, (c + 1) * part)
        own = covariance(owned[c], mask[span], scale[None, span], group)
        covs.append(
            [
                lax.ppermute(own, "segment", [(k, k + d) for k in range(segments - d)])
                for d in range(1, segments)
            ]
        )
    result = None
    for c in range(chunks):
        result = beams(covs[c], owned[c], steer_pair, steer, comp, result, c, bins, group)
    return result


def solution(mesh):
    in_specs = (
        P("segment", "blk", None, None),
        P("segment", "blk", None),
        P("segment", "blk"),
        P(),
        P(),
    )
    out_specs = P("segment", "blk", None, None)
    return jax.shard_map(local, mesh=mesh, in_specs=in_specs, out_specs=out_specs, check_vma=False)
```

time: 964 us -> 345 us (0.36)
  matrix products: 462 us -> 2.65 us
  waiting for transfers between devices: 324 us -> 146 us
  Pallas kernels: 0 us -> 124 us
  other arithmetic: 52.3 us -> 1.78 us
  local copies, waits for them, and re-layouts: 69.6 us -> 24 us
  starting transfers between devices: 6.5 us -> 45.5 us
  loops' own time: 18.4 us -> 0 us
  between operations: 13.8 us -> 0.47 us
  blocking collectives: 10.3 us -> 0 us
    dot_general x105 -> x1, matrix products: 462 us -> 2.65 us  [compression_rows(): table = jnp.einsum('pql,kl->kpq', onehot, code_table, precision=highest)]
    all_gather x1 -> x0, waiting for transfers between devices: 141 us -> none  [entering(): pieces = jax.tree.map(lambda part: lax.all_gather(part, axis), value)]
    pallas_call x0 -> x12, Pallas kernels: none -> 124 us  [the longest x4 100 us: beams(): pl.pallas_call(functools.partial(beam_kernel, len(covs), NS_STEPS), grid=...]
    all_to_all x1 -> x4, waiting for transfers between devices: 183 us -> 146 us  [local(): lax.all_to_all(spectra, 'blk', split_axis=0, concat_axis=0, tiled=True)]
    ppermute x0 -> x12, starting transfers between devices: none -> 28.2 us  [local(): lax.ppermute(own, 'segment', [(k, k + d) for k in range(segments - d)])]
    while x60 -> x0, local copies, waits for them, and re-layouts: 26.5 us -> none
    unnamed x13 -> x41, local copies, waits for them, and re-layouts: 2.06 us -> 22.9 us
    select_n x3 -> x0, other arithmetic: 19.9 us -> none  [turn(): jnp.where(position < mine, new, old)]
  transfers between devices with their start and end apart: 2 -> 16, of which waited for: 2 -> 4; matrix products, arithmetic and copies ran while one was open for 1% -> 1% of each run, Pallas kernels for 0% -> 28%
where the time goes in v1:
time: 345 us
  waiting for transfers between devices  146 us (42%)
  Pallas kernels  124 us (36%)
  starting transfers between devices  45.5 us (13%)
  local copies, waits for them, and re-layouts  24 us (7%)
    all_to_all x4, waiting for transfers between devices, local(): lax.all_to_all(spectra, 'blk', split_axis=0, concat_axis=0, tiled=True)  146 us
    pallas_call x4, Pallas kernels, beams(): pl.pallas_call(functools.partial(beam_kernel, len(covs), NS_STEPS), grid=...  100 us
    ppermute x12, starting transfers between devices, local(): lax.ppermute(own, 'segment', [(k, k + d) for k in range(segments - d)])  28.2 us
    unnamed x41, local copies, waits for them, and re-layouts  22.9 us
    all_to_all x4, starting transfers between devices, local(): lax.all_to_all(spectra, 'blk', split_axis=0, concat_axis=0, tiled=True)  17.3 us
    pallas_call x4, Pallas kernels, doppler(): pl.pallas_call(doppler_kernel, grid=(ranges // rows,), in_specs=[pl.Block...  16 us
    pallas_call x4, Pallas kernels, covariance(): pl.pallas_call(covariance_kernel, grid=(bins // group,), in_specs=[pl.Blo...  7.54 us
  transfers between devices with their start and end apart: 16, of which 4 were waited for; matrix products, arithmetic and copies ran while one was open for 1% of the time, Pallas kernels for 28%

profile of v1, /device:TPU:0, one launch (start us, length us, event | category | flops | bytes accessed | tf_op | source)
XLA Modules:
  0.0 344.6 jit_solution(9483363724005424970)
XLA Ops:
  2.2 3.4 copy-done
  5.6 4.0 %shard_map.61 = bf16[64,64,256]{2,1,0:T(8,128)(2,1)S(1)} custom-call(bf16[64,128,512]{2,1,0:T(8,128)(2,1)S(1)} %bitcast.32, bf16[128,512]{1,0:T(8,128)(2,1)S(1)} %bitcast.43), custom_call_target="tpu_custom_call" | custom-call | flops 1073741824 | bytes 10485760 | tf_op jit(solution)/shard_map/pallas_call | solution.py:80
  10.9 6.3 %all-to-all-start.3 = ((bf16[8,8,64,256]{3,2,1,0:T(8,128)(2,1)}), bf16[8,8,64,256]{3,2,1,0:T(8,128)(2,1)S(1)}, u32[]{:S(2)}, u32[]{:S(2)}) async-start(bf16[8,8,64,256]{3,2,1,0:T(8,128)(2,1)} %bitcast.39), calls=%async_computation.3 | async-start | bytes 4194304 | tf_op jit(solution)/shard_map/all_to_all | solution.py:288
  17.2 3.4 copy-done.1
  20.6 4.0 %shard_map.59 = bf16[64,64,256]{2,1,0:T(8,128)(2,1)S(1)} custom-call(bf16[64,128,512]{2,1,0:T(8,128)(2,1)S(1)} %bitcast.33, bf16[128,512]{1,0:T(8,128)(2,1)S(1)} %bitcast.42), custom_call_target="tpu_custom_call" | custom-call | flops 1073741824 | bytes 10485760 | tf_op jit(solution)/shard_map/pallas_call | solution.py:80
  25.9 40.4 %all-to-all-done.3.y_ref.refs_3_ = bf16[8,8,64,256]{3,2,1,0:T(8,128)(2,1)S(1)} async-done(((bf16[8,8,64,256]{3,2,1,0:T(8,128)(2,1)}), bf16[8,8,64,256]{3,2,1,0:T(8,128)(2,1)S(1)}, u32[]{:S(2)}, u32[]{:S(2)}) %all-to-all-start.3) | async-done | bytes 2097184 | tf_op jit(solution)/shard_map/all_to_all | solution.py:288
  67.7 3.6 %all-to-all-start.2 = ((bf16[8,8,64,256]{3,2,1,0:T(8,128)(2,1)}), bf16[8,8,64,256]{3,2,1,0:T(8,128)(2,1)S(1)}, u32[]{:S(2)}, u32[]{:S(2)}) async-start(bf16[8,8,64,256]{3,2,1,0:T(8,128)(2,1)} %bitcast.38), calls=%async_computation.2 | async-start | bytes 4194304 | tf_op jit(solution)/shard_map/all_to_all | solution.py:288
  71.3 3.4 copy-done.2
  74.7 4.0 %shard_map.57 = bf16[64,64,256]{2,1,0:T(8,128)(2,1)S(1)} custom-call(bf16[64,128,512]{2,1,0:T(8,128)(2,1)S(1)} %bitcast.34, bf16[128,512]{1,0:T(8,128)(2,1)S(1)} %bitcast.41), custom_call_target="tpu_custom_call" | custom-call | flops 1073741824 | bytes 10485760 | tf_op jit(solution)/shard_map/pallas_call | solution.py:80
  80.0 40.2 %all-to-all-done.2.y_ref.refs_3_ = bf16[8,8,64,256]{3,2,1,0:T(8,128)(2,1)S(1)} async-done(((bf16[8,8,64,256]{3,2,1,0:T(8,128)(2,1)}), bf16[8,8,64,256]{3,2,1,0:T(8,128)(2,1)S(1)}, u32[]{:S(2)}, u32[]{:S(2)}) %all-to-all-start.2) | async-done | bytes 2097184 | tf_op jit(solution)/shard_map/all_to_all | solution.py:288
  121.6 3.6 %all-to-all-start.1 = ((bf16[8,8,64,256]{3,2,1,0:T(8,128)(2,1)}), bf16[8,8,64,256]{3,2,1,0:T(8,128)(2,1)S(1)}, u32[]{:S(2)}, u32[]{:S(2)}) async-start(bf16[8,8,64,256]{3,2,1,0:T(8,128)(2,1)} %bitcast.37), calls=%async_computation.1 | async-start | bytes 4194304 | tf_op jit(solution)/shard_map/all_to_all | solution.py:288
  125.2 3.4 copy-done.3
  128.6 4.0 %shard_map.55 = bf16[64,64,256]{2,1,0:T(8,128)(2,1)S(1)} custom-call(bf16[64,128,512]{2,1,0:T(8,128)(2,1)S(1)} %bitcast.35, bf16[128,512]{1,0:T(8,128)(2,1)S(1)} %bitcast.40), custom_call_target="tpu_custom_call" | custom-call | flops 1073741824 | bytes 10485760 | tf_op jit(solution)/shard_map/pallas_call | solution.py:80
  133.9 40.3 %all-to-all-done.1.y_ref.refs_3_ = bf16[8,8,64,256]{3,2,1,0:T(8,128)(2,1)S(1)} async-done(((bf16[8,8,64,256]{3,2,1,0:T(8,128)(2,1)}), bf16[8,8,64,256]{3,2,1,0:T(8,128)(2,1)S(1)}, u32[]{:S(2)}, u32[]{:S(2)}) %all-to-all-start.1) | async-done | bytes 2097184 | tf_op jit(solution)/shard_map/all_to_all | solution.py:288
  175.6 3.7 %all-to-all-start = ((bf16[8,8,64,256]{3,2,1,0:T(8,128)(2,1)}), bf16[8,8,64,256]{3,2,1,0:T(8,128)(2,1)S(1)}, u32[]{:S(2)}, u32[]{:S(2)}) async-start(bf16[8,8,64,256]{3,2,1,0:T(8,128)(2,1)} %bitcast.36), calls=%async_computation | async-start | bytes 4194304 | tf_op jit(solution)/shard_map/all_to_all | solution.py:288
  179.6 2.6 fusion.2
  184.1 4.4 %collective-permute-start.10 = (f32[8,128,128]{2,1,0:T(8,128)S(1)}, f32[8,128,128]{2,1,0:T(8,128)}, u32[]{:S(2)}, u32[]{:S(2)}) collective-permute-start(f32[8,128,128]{2,1,0:T(8,128)S(1)} %shard_map.62), channel_id=1, source_target_pairs={{0,16},{8,24},{1,17},{9,25},{2,18},{10,26},{3,19},{11,27},{4,20},{... | collective-permute-start | bytes 1572872 | tf_op jit(solution)/shard_map/ppermute | solution.py:294
  190.8 3.5 %collective-permute-start.9 = (f32[8,128,128]{2,1,0:T(8,128)S(1)}, f32[8,128,128]{2,1,0:T(8,128)}, u32[]{:S(2)}, u32[]{:S(2)}) collective-permute-start(f32[8,128,128]{2,1,0:T(8,128)S(1)} %shard_map.62), channel_id=1, source_target_pairs={{0,8},{8,16},{16,24},{1,9},{9,17},{17,25},{2,10},{10,18},{18,26},{... | collective-permute-start | bytes 1572872 | tf_op jit(solution)/shard_map/ppermute | solution.py:294
  202.9 25.4 %all-to-all-done.y_ref.refs_3_ = bf16[8,8,64,256]{3,2,1,0:T(8,128)(2,1)S(1)} async-done(((bf16[8,8,64,256]{3,2,1,0:T(8,128)(2,1)}), bf16[8,8,64,256]{3,2,1,0:T(8,128)(2,1)S(1)}, u32[]{:S(2)}, u32[]{:S(2)}) %all-to-all-start) | async-done | bytes 2097184 | tf_op jit(solution)/shard_map/all_to_all | solution.py:288
  230.0 4.4 %collective-permute-start.8 = (f32[8,128,128]{2,1,0:T(8,128)}, f32[8,128,128]{2,1,0:T(8,128)S(1)}, u32[]{:S(2)}, u32[]{:S(2)}) collective-permute-start(f32[8,128,128]{2,1,0:T(8,128)} %shard_map.60), channel_id=1, source_target_pairs={{0,24},{1,25},{2,26},{3,27},{4,28},{5,29},{6,30},{7,31}} | collective-permute-start | bytes 1572872 | tf_op jit(solution)/shard_map/ppermute | solution.py:294
  238.4 25.7 %shard_map.63.refs_7_ = bf16[1,32,512,256]{3,2,1,0:T(8,128)(2,1)} custom-call(f32[8,128,128]{2,1,0:T(8,128)} %collective-permute-done.9.refs_0_, f32[8,128,128]{2,1,0:T(8,128)} %collective-permute-done.10.refs_1_, f32[8,128,128]{2,1,0:T(8,128)} %collective-permute-done.11.refs_2_, bf16[8,8,64,256]{3,2,1,0:T(8,128)(2,1)S(1)} %copy-done.12, ...), custom_call_target="tpu_custom_call" | custom-call | flops 25769803776 | bytes 4194304 | tf_op jit(solution)/shard_map/pallas_call | solution.py:234
  268.3 25.5 %shard_map.64.refs_7_ = bf16[1,32,512,256]{3,2,1,0:T(8,128)(2,1)} custom-call(f32[8,128,128]{2,1,0:T(8,128)} %collective-permute-done.6.refs_0_, f32[8,128,128]{2,1,0:T(8,128)} %collective-permute-done.7.refs_1_, f32[8,128,128]{2,1,0:T(8,128)S(1)} %collective-permute-done.8.refs_2_, ...), custom_call_target="tpu_custom_call", output_to_operand_aliasing={{}: (7, {})} | custom-call | flops 25769803776 | bytes 4194304 | tf_op jit(solution)/shard_map/pallas_call | solution.py:234
  295.3 24.6 %shard_map.65.refs_7_ = bf16[1,32,512,256]{3,2,1,0:T(8,128)(2,1)} custom-call(f32[8,128,128]{2,1,0:T(8,128)S(1)} %collective-permute-done.3.refs_0_, f32[8,128,128]{2,1,0:T(8,128)S(1)} %collective-permute-done.4.refs_1_, f32[8,128,128]{2,1,0:T(8,128)S(1)} %collective-permute-done.5.refs_2_, ...), custom_call_target="tpu_custom_call", output_to_operand_aliasing={{}: (7, {})} | custom-call | flops 25769803776 | bytes 4194304 | tf_op jit(solution)/shard_map/pallas_call | solution.py:234
  320.0 24.6 %shard_map.66 = bf16[1,32,512,256]{3,2,1,0:T(8,128)(2,1)} custom-call(f32[8,128,128]{2,1,0:T(8,128)S(1)} %collective-permute-done.refs_0_, f32[8,128,128]{2,1,0:T(8,128)S(1)} %collective-permute-done.1.refs_1_, f32[8,128,128]{2,1,0:T(8,128)S(1)} %collective-permute-done.2.refs_2_, ...), custom_call_target="tpu_custom_call", output_to_operand_aliasing={{}: (7, {})} | custom-call | flops 25769803776 | bytes 4194304 | tf_op jit(solution)/shard_map/pallas_call | solution.py:234
  (83 shorter events, 35.8 us)
Async XLA Ops:
  10.9 55.4 %all-to-all-start.3 = ((bf16[8,8,64,256]{3,2,1,0:T(8,128)(2,1)}), bf16[8,8,64,256]{3,2,1,0:T(8,128)(2,1)S(1)}, u32[]{:S(2)}, u32[]{:S(2)}) async-start(bf16[8,8,64,256]{3,2,1,0:T(8,128)(2,1)} %bitcast.39), calls=%async_computation.3 | async-start | bytes 4194304 | tf_op jit(solution)/shard_map/all_to_all | solution.py:288
  67.7 52.6 %all-to-all-start.2 = ((bf16[8,8,64,256]{3,2,1,0:T(8,128)(2,1)}), bf16[8,8,64,256]{3,2,1,0:T(8,128)(2,1)S(1)}, u32[]{:S(2)}, u32[]{:S(2)}) async-start(bf16[8,8,64,256]{3,2,1,0:T(8,128)(2,1)} %bitcast.38), calls=%async_computation.2 | async-start | bytes 4194304 | tf_op jit(solution)/shard_map/all_to_all | solution.py:288
  121.6 52.6 %all-to-all-start.1 = ((bf16[8,8,64,256]{3,2,1,0:T(8,128)(2,1)}), bf16[8,8,64,256]{3,2,1,0:T(8,128)(2,1)S(1)}, u32[]{:S(2)}, u32[]{:S(2)}) async-start(bf16[8,8,64,256]{3,2,1,0:T(8,128)(2,1)} %bitcast.37), calls=%async_computation.1 | async-start | bytes 4194304 | tf_op jit(solution)/shard_map/all_to_all | solution.py:288
  175.5 3.8 %copy-start.17 = (s32[1,32,6]{1,0,2:T(1,128)S(1)}, s32[1,32,6]{1,0,2:T(1,128)}, u32[]{:S(2)}) copy-start(s32[1,32,6]{1,0,2:T(1,128)} %param.6) | copy-start | bytes 2308
  175.5 3.8 %copy-start.19 = (s32[1,32]{1,0:T(1,128)S(1)}, s32[1,32]{1,0:T(1,128)}, u32[]{:S(2)}) copy-start(s32[1,32]{1,0:T(1,128)} %param.7) | copy-start | bytes 388
  175.5 4.0 %copy-start.18 = (f32[64]{0:T(128)S(1)}, f32[64]{0:T(128)}, u32[]{:S(2)}) copy-start(f32[64]{0:T(128)} %param.9) | copy-start | bytes 772
  175.6 52.7 %all-to-all-start = ((bf16[8,8,64,256]{3,2,1,0:T(8,128)(2,1)}), bf16[8,8,64,256]{3,2,1,0:T(8,128)(2,1)S(1)}, u32[]{:S(2)}, u32[]{:S(2)}) async-start(bf16[8,8,64,256]{3,2,1,0:T(8,128)(2,1)} %bitcast.36), calls=%async_computation | async-start | bytes 4194304 | tf_op jit(solution)/shard_map/all_to_all | solution.py:288
  182.3 12.3 %copy-start.8 = (bf16[8,8,64,256]{3,2,1,0:T(8,128)(2,1)S(1)}, bf16[8,8,64,256]{3,2,1,0:T(8,128)(2,1)}, u32[]{:S(2)}) copy-start(bf16[8,8,64,256]{3,2,1,0:T(8,128)(2,1)} %copy-done.7) | copy-start | bytes 6291460
  184.1 17.1 %copy-start.5 = (bf16[8,8,64,256]{3,2,1,0:T(8,128)(2,1)S(1)}, bf16[8,8,64,256]{3,2,1,0:T(8,128)(2,1)}, u32[]{:S(2)}) copy-start(bf16[8,8,64,256]{3,2,1,0:T(8,128)(2,1)} %copy-done.4) | copy-start | bytes 6291460
  184.1 45.9 %collective-permute-start.10 = (f32[8,128,128]{2,1,0:T(8,128)S(1)}, f32[8,128,128]{2,1,0:T(8,128)}, u32[]{:S(2)}, u32[]{:S(2)}) collective-permute-start(f32[8,128,128]{2,1,0:T(8,128)S(1)} %shard_map.62), channel_id=1, source_target_pairs={{0,16},{8,24},{1,17},{9,25},{2,18},{10,26},{3,19},{11,27},{4,20},{... | collective-permute-start | bytes 1572872 | tf_op jit(solution)/shard_map/ppermute | solution.py:294
  188.6 45.8 %collective-permute-start.11 = (f32[8,128,128]{2,1,0:T(8,128)S(1)}, f32[8,128,128]{2,1,0:T(8,128)}, u32[]{:S(2)}, u32[]{:S(2)}) collective-permute-start(f32[8,128,128]{2,1,0:T(8,128)S(1)} %shard_map.62), channel_id=1, source_target_pairs={{0,24},{1,25},{2,26},{3,27},{4,28},{5,29},{6,30},{7,31}} | collective-permute-start | bytes 1572872 | tf_op jit(solution)/shard_map/ppermute | solution.py:294
  190.8 45.0 %collective-permute-start.9 = (f32[8,128,128]{2,1,0:T(8,128)S(1)}, f32[8,128,128]{2,1,0:T(8,128)}, u32[]{:S(2)}, u32[]{:S(2)}) collective-permute-start(f32[8,128,128]{2,1,0:T(8,128)S(1)} %shard_map.62), channel_id=1, source_target_pairs={{0,8},{8,16},{16,24},{1,9},{9,17},{17,25},{2,10},{10,18},{18,26},{... | collective-permute-start | bytes 1572872 | tf_op jit(solution)/shard_map/ppermute | solution.py:294
  197.0 67.1 %collective-permute-start.6 = (f32[8,128,128]{2,1,0:T(8,128)}, f32[8,128,128]{2,1,0:T(8,128)}, u32[]{:S(2)}, u32[]{:S(2)}) collective-permute-start(f32[8,128,128]{2,1,0:T(8,128)} %shard_map.60), channel_id=1, source_target_pairs={{0,8},{8,16},{16,24},{1,9},{9,17},{17,25},{2,10},{10,18},{18,26},{... | collective-permute-start | bytes 1572872 | tf_op jit(solution)/shard_map/ppermute | solution.py:294
  199.1 66.5 %collective-permute-start.7 = (f32[8,128,128]{2,1,0:T(8,128)}, f32[8,128,128]{2,1,0:T(8,128)}, u32[]{:S(2)}, u32[]{:S(2)}) collective-permute-start(f32[8,128,128]{2,1,0:T(8,128)} %shard_map.60), channel_id=1, source_target_pairs={{0,16},{8,24},{1,17},{9,25},{2,18},{10,26},{3,19},{11,27},{4,20},{... | collective-permute-start | bytes 1572872 | tf_op jit(solution)/shard_map/ppermute | solution.py:294
  228.3 10.1 %copy-start.12 = (bf16[8,8,64,256]{3,2,1,0:T(8,128)(2,1)S(1)}, bf16[8,8,64,256]{3,2,1,0:T(8,128)(2,1)}, u32[]{:S(2)}) copy-start(bf16[8,8,64,256]{3,2,1,0:T(8,128)(2,1)} %copy-done.10) | copy-start | bytes 6291460
  230.0 36.9 %collective-permute-start.8 = (f32[8,128,128]{2,1,0:T(8,128)}, f32[8,128,128]{2,1,0:T(8,128)S(1)}, u32[]{:S(2)}, u32[]{:S(2)}) collective-permute-start(f32[8,128,128]{2,1,0:T(8,128)} %shard_map.60), channel_id=1, source_target_pairs={{0,24},{1,25},{2,26},{3,27},{4,28},{5,29},{6,30},{7,31}} | collective-permute-start | bytes 1572872 | tf_op jit(solution)/shard_map/ppermute | solution.py:294
  234.4 59.4 %collective-permute-start.3 = (f32[8,128,128]{2,1,0:T(8,128)S(1)}, f32[8,128,128]{2,1,0:T(8,128)S(1)}, u32[]{:S(2)}, u32[]{:S(2)}) collective-permute-start(f32[8,128,128]{2,1,0:T(8,128)S(1)} %shard_map.58), channel_id=1, source_target_pairs={{0,8},{8,16},{16,24},{1,9},{9,17},{17,25},{2,10},{10,18},{18,26},{... | collective-permute-start | bytes 1572872 | tf_op jit(solution)/shard_map/ppermute | solution.py:294
  235.7 59.6 %collective-permute-start.4 = (f32[8,128,128]{2,1,0:T(8,128)S(1)}, f32[8,128,128]{2,1,0:T(8,128)S(1)}, u32[]{:S(2)}, u32[]{:S(2)}) collective-permute-start(f32[8,128,128]{2,1,0:T(8,128)S(1)} %shard_map.58), channel_id=1, source_target_pairs={{0,16},{8,24},{1,17},{9,25},{2,18},{10,26},{3,19},{11,27},{4,20},{... | collective-permute-start | bytes 1572872 | tf_op jit(solution)/shard_map/ppermute | solution.py:294
  238.4 29.9 %copy-start.9 = (bf16[8,8,64,256]{3,2,1,0:T(8,128)(2,1)S(1)}, bf16[8,8,64,256]{3,2,1,0:T(8,128)(2,1)}, u32[]{:S(2)}) copy-start(bf16[8,8,64,256]{3,2,1,0:T(8,128)(2,1)} %copy-done.7) | copy-start | bytes 6291460
  264.1 31.2 %copy-start.6 = (bf16[8,8,64,256]{3,2,1,0:T(8,128)(2,1)S(1)}, bf16[8,8,64,256]{3,2,1,0:T(8,128)(2,1)}, u32[]{:S(2)}) copy-start(bf16[8,8,64,256]{3,2,1,0:T(8,128)(2,1)} %copy-done.4) | copy-start | bytes 6291460
  264.1 31.2 %collective-permute-start.5 = (f32[8,128,128]{2,1,0:T(8,128)S(1)}, f32[8,128,128]{2,1,0:T(8,128)S(1)}, u32[]{:S(2)}, u32[]{:S(2)}) collective-permute-start(f32[8,128,128]{2,1,0:T(8,128)S(1)} %shard_map.58), channel_id=1, source_target_pairs={{0,24},{1,25},{2,26},{3,27},{4,28},{5,29},{6,30},{7,31}} | collective-permute-start | bytes 1572872 | tf_op jit(solution)/shard_map/ppermute | solution.py:294
  265.6 54.4 %collective-permute-start = (f32[8,128,128]{2,1,0:T(8,128)S(1)}, f32[8,128,128]{2,1,0:T(8,128)S(1)}, u32[]{:S(2)}, u32[]{:S(2)}) collective-permute-start(f32[8,128,128]{2,1,0:T(8,128)S(1)} %shard_map.56), channel_id=1, source_target_pairs={{0,8},{8,16},{16,24},{1,9},{9,17},{17,25},{2,10},{10,18},{18,26},{... | collective-permute-start | bytes 1572872 | tf_op jit(solution)/shard_map/ppermute | solution.py:294
  266.9 53.0 %collective-permute-start.1 = (f32[8,128,128]{2,1,0:T(8,128)S(1)}, f32[8,128,128]{2,1,0:T(8,128)S(1)}, u32[]{:S(2)}, u32[]{:S(2)}) collective-permute-start(f32[8,128,128]{2,1,0:T(8,128)S(1)} %shard_map.56), channel_id=1, source_target_pairs={{0,16},{8,24},{1,17},{9,25},{2,18},{10,26},{3,19},{11,27},{4,20},{... | collective-permute-start | bytes 1572872 | tf_op jit(solution)/shard_map/ppermute | solution.py:294
  293.8 26.2 %collective-permute-start.2 = (f32[8,128,128]{2,1,0:T(8,128)S(1)}, f32[8,128,128]{2,1,0:T(8,128)S(1)}, u32[]{:S(2)}, u32[]{:S(2)}) collective-permute-start(f32[8,128,128]{2,1,0:T(8,128)S(1)} %shard_map.56), channel_id=1, source_target_pairs={{0,24},{1,25},{2,26},{3,27},{4,28},{5,29},{6,30},{7,31}} | collective-permute-start | bytes 1572872 | tf_op jit(solution)/shard_map/ppermute | solution.py:294
  (12 other events, 25.8 us)

commit v2 on v1

--- a/solution.py
+++ b/solution.py
@@ -14,8 +14,9 @@
 NTR_EASY = 3
 NS_STEPS = 12
 CBLK = 128
-CHUNKS = 4
+SHARES = (3, 2, 2, 1)
 GROUP = 4
+SHORT_STEPS = 3
 
 decay_rate = 0.7
 diag_load = 0.1
@@ -54,7 +55,8 @@
     return table.reshape(2 * block_len, 2 * block_len).astype(bf16)
 
 
-def doppler_kernel(x_ref, t_ref, o_ref, scr):
+def doppler_kernel(x_ref, t_ref, *refs):
+    o_ref, scr = refs[-2:]
     rows, channels, _ = x_ref.shape
     slots = o_ref.shape[0]
     pair = 2
@@ -73,7 +75,7 @@
         )
 
 
-def doppler(samples, table):
+def doppler(samples, table, after):
     ranges, channels, width = samples.shape
     slots = table.shape[0] // 2
     rows = 16
@@ -83,17 +85,18 @@
         in_specs=[
             pl.BlockSpec((rows, channels, width), lambda i: (i, 0, 0)),
             pl.BlockSpec(table.shape, lambda i: (0, 0)),
+            *[pl.BlockSpec(memory_space=pl.ANY) for _ in after],
         ],
         out_specs=pl.BlockSpec((slots, rows, 2 * channels), lambda i: (0, i, 0)),
         out_shape=jax.ShapeDtypeStruct((slots, ranges, 2 * channels), bf16),
         scratch_shapes=[pltpu.VMEM((2, slots * rows, channels), f32)],
-        compiler_params=pltpu.CompilerParams(vmem_limit_bytes=40 * 2**20),
+        compiler_params=pltpu.CompilerParams(vmem_limit_bytes=60 * 2**20),
         cost_estimate=pl.CostEstimate(
             flops=4 * ranges * channels * width * slots,
             bytes_accessed=2 * samples.size + 4 * slots * ranges * channels,
             transcendentals=0,
         ),
-    )(samples, table)
+    )(samples, table, *after)
 
 
 def covariance_kernel(m_ref, s_ref, y_ref, o_ref):
@@ -161,23 +164,24 @@
 
 
 def product(left_pair, right_pair):
-    n = left_pair.shape[0] // 2
+    n = right_pair.shape[0]
     ch = right_pair.shape[1] // 2
     p = jnp.dot(left_pair, right_pair, preferred_element_type=f32)
-    return p[:n, :ch] + (p[:n, ch:] + p[n:, :ch])
+    total = p[:n, :ch] + p[:n, ch:]
+    return total if left_pair.shape[0] == n else total + p[n:, :ch]
 
 
 def beam_kernel(terms, steps, *refs):
     cov_refs = refs[:terms]
     y_ref, sp_ref, st_ref, c_ref = refs[terms : terms + 4]
-    o_ref, a_scr, x_scr = refs[-3:]
+    o_ref, done_ref, a_scr, x_scr = refs[-4:]
+    done_ref[...] = jnp.zeros_like(done_ref)
     sources, group, rows, width = y_ref.shape
     ch = width // 2
     ranges = sources * rows
     row = lax.broadcasted_iota(jnp.int32, (ch, ch), 0)
     col = lax.broadcasted_iota(jnp.int32, (ch, ch), 1)
     eye = (row == col).astype(f32)
-    two_eye = jnp.concatenate([2.0 * eye, jnp.zeros_like(eye)], axis=0)
     for g in range(group):
         packed = cov_refs[0][g]
         for d in range(1, terms):
@@ -187,16 +191,19 @@
         im = jnp.where(row > col, packed, jnp.where(row < col, -flipped, 0.0))
         trace_value = jnp.sum(jnp.sum(re * eye, axis=1, keepdims=True), axis=0, keepdims=True)
         a_scr[g] = left(jnp.concatenate([re, im], axis=0))
-        x_scr[g] = jnp.concatenate([eye / trace_value, jnp.zeros_like(eye)], axis=0)
-
-    def newton(step, carry):
+        x_scr[g] = jnp.concatenate([2.0 * eye - re / trace_value, -im / trace_value], axis=0) / trace_value
+
+    def newton(depth, step, carry):
         held = [x_scr[g] for g in range(group)]
-        middle = [two_eye - product(a_scr[g], right(held[g])) for g in range(group)]
+        pairs = [right(x) for x in held]
+        middle = [product(a_scr[g, :depth], pairs[g]) for g in range(group)]
         for g in range(group):
-            x_scr[g] = product(left(held[g]), right(middle[g]))
+            x_scr[g] = 2.0 * held[g] - product(full(pairs[g][:, :ch]), right(middle[g]))
         return carry
 
-    lax.fori_loop(0, steps, newton, 0)
+    short = min(SHORT_STEPS, steps - 1)
+    lax.fori_loop(0, short, functools.partial(newton, 2 * ch), 0)
+    lax.fori_loop(short, steps - 1, functools.partial(newton, 4 * ch), 0)
     for g in range(group):
         vec = product(left(x_scr[g]), sp_ref[...])
         gain = jnp.sum(st_ref[...] * vec, axis=0, keepdims=True)
@@ -213,12 +220,12 @@
             o_ref[g, base : base + CBLK, :] = jnp.concatenate([out_re, out_im], axis=1).astype(bf16)
 
 
-def beams(covs, owned, steer_pair, steer, comp, earlier, chunk, total_bins, group):
+def beams(covs, owned, steer_pair, steer, comp, earlier, start, total_bins, group):
     sources, bins, rows, width = owned.shape
     ch = width // 2
     ranges = sources * rows
     steps = bins // group
-    offset = chunk * steps
+    offset = start // group
     in_specs = [pl.BlockSpec((group, ch, ch), lambda i: (i, 0, 0)) for _ in covs] + [
         pl.BlockSpec((sources, group, rows, width), lambda i: (0, i, 0, 0)),
         pl.BlockSpec(steer_pair.shape, lambda i: (0, 0)),
@@ -235,8 +242,14 @@
         functools.partial(beam_kernel, len(covs), NS_STEPS),
         grid=(steps,),
         in_specs=in_specs,
-        out_specs=pl.BlockSpec((None, group, ranges, width), lambda i: (0, offset + i, 0, 0)),
-        out_shape=jax.ShapeDtypeStruct((1, total_bins, ranges, width), bf16),
+        out_specs=[
+            pl.BlockSpec((None, group, ranges, width), lambda i: (0, offset + i, 0, 0)),
+            pl.BlockSpec((8, 128), lambda i: (0, 0)),
+        ],
+        out_shape=[
+            jax.ShapeDtypeStruct((1, total_bins, ranges, width), bf16),
+            jax.ShapeDtypeStruct((8, 128), f32),
+        ],
         scratch_shapes=[
             pltpu.VMEM((group, 4 * ch, 2 * ch), bf16),
             pltpu.VMEM((group, 2 * ch, ch), f32),
@@ -244,7 +257,7 @@
         input_output_aliases=aliases,
         compiler_params=pltpu.CompilerParams(vmem_limit_bytes=48 * 2**20),
         cost_estimate=pl.CostEstimate(
-            flops=bins * (2 * NS_STEPS * 2 * 4 * ch * 4 * ch * ch * 2),
+            flops=bins * (3 * NS_STEPS * 4 * ch * 4 * ch * ch),
             bytes_accessed=4 * owned.size,
             transcendentals=0,
         ),
@@ -258,14 +271,15 @@
     segments = lax.axis_size("segment")
     blocks, hard = train_blocks[0], hard_bins[0]
     bins, listed = blocks.shape
-    chunks = CHUNKS
-    while bins % chunks:
-        chunks //= 2
-    part = bins // chunks
-    group = math.gcd(part, GROUP)
+    unit = bins // sum(SHARES)
+    shares = [unit * share for share in SHARES]
+    shares[-1] += bins - sum(shares)
+    shares = [share for share in shares if share > 0]
+    starts = [sum(shares[:c]) for c in range(len(shares))]
+    chunks = len(shares)
 
     table = doppler_rows(owner_map, double_pulses // 2).reshape(
-        2, owners, chunks, part, double_pulses
+        2, owners, bins, double_pulses
     )
     keep = (jnp.arange(listed, dtype=jnp.int32)[None, :] < NTR_EASY) | (hard[:, None] == 1)
     total_blocks = owners * ranges_local // RB
@@ -281,23 +295,45 @@
     steer_pair = jnp.concatenate([steer_hi.astype(bf16), (steer - steer_hi).astype(bf16)], axis=1)
     comp = compression_rows(code_phase, CBLK)
 
+    groups = [math.gcd(math.gcd(share, GROUP), start) for share, start in zip(shares, starts)]
     owned, covs = [], []
-    for c in range(chunks):
-        spectra = doppler(samples, table[:, :, c].reshape(2 * owners * part, double_pulses))
-        spectra = spectra.reshape(owners, part, ranges_local, 2 * channels)
+    result = None
+
+    def send(c, after):
+        span = slice(starts[c], starts[c] + shares[c])
+        rows = table[:, :, span].reshape(2 * owners * shares[c], double_pulses)
+        spectra = doppler(samples, rows, after)
+        spectra = spectra.reshape(owners, shares[c], ranges_local, 2 * channels)
         owned.append(lax.all_to_all(spectra, "blk", split_axis=0, concat_axis=0, tiled=True))
-    for c in range(chunks):
-        span = slice(c * part, (c + 1) * part)
-        own = covariance(owned[c], mask[span], scale[None, span], group)
+        return spectra
+
+    def exchange(c):
+        span = slice(starts[c], starts[c] + shares[c])
+        own = covariance(owned[c], mask[span], scale[None, span], groups[c])
         covs.append(
             [
                 lax.ppermute(own, "segment", [(k, k + d) for k in range(segments - d)])
                 for d in range(1, segments)
             ]
         )
-    result = None
+        return covs[c]
+
+    def form(c, earlier):
+        return beams(
+            covs[c], owned[c], steer_pair, steer, comp, earlier, starts[c], bins, groups[c]
+        )
+
+    first = send(0, ())
+    if chunks > 1:
+        send(1, [first])
     for c in range(chunks):
-        result = beams(covs[c], owned[c], steer_pair, steer, comp, result, c, bins, group)
+        after = [*exchange(c)]
+        if c > 0:
+            result, done = form(c - 1, result)
+            after.append(done)
+        if c + 2 < chunks:
+            send(c + 2, after)
+    result, _ = form(chunks - 1, result)
     return result
 
 

time: 345 us -> 283 us (0.82)
  waiting for transfers between devices: 146 us -> 92.1 us
  local copies, waits for them, and re-layouts: 24 us -> 6.73 us
  starting transfers between devices: 45.5 us -> 51.6 us
    all_to_all x4, waiting for transfers between devices: 146 us -> 63.5 us  [send(): lax.all_to_all(spectra, 'blk', split_axis=0, concat_axis=0, tiled=True)]
    ppermute x12, waiting for transfers between devices: 0.03 us -> 28.5 us  [exchange(): lax.ppermute(own, 'segment', [(k, k + d) for k in range(segments - d)])]
    unnamed x41 -> x17, local copies, waits for them, and re-layouts: 22.9 us -> 2.01 us
    pallas_call x4, Pallas kernels: 16 us -> 29 us  [doppler(): pl.pallas_call(doppler_kernel, grid=(ranges // rows,), in_specs=[pl.Block...]
    pallas_call x4, Pallas kernels: 100 us -> 87.4 us  [beams(): pl.pallas_call(functools.partial(beam_kernel, len(covs), NS_STEPS), grid=...]
    all_to_all x4, starting transfers between devices: 17.3 us -> 20.8 us  [send(): lax.all_to_all(spectra, 'blk', split_axis=0, concat_axis=0, tiled=True)]
  transfers between devices with their start and end apart: 16 -> 16, of which waited for: 4 -> 3; matrix products, arithmetic and copies ran while one was open for 1% -> 3% of each run, Pallas kernels for 28% -> 38%
where the time goes in v2:
time: 283 us; the launch traced here: 282 us
  Pallas kernels  124 us (44%)
  waiting for transfers between devices  92.1 us (33%)
  starting transfers between devices  51.6 us (18%)
  local copies, waits for them, and re-layouts  6.73 us (2%)
  other arithmetic  4.03 us (1%)
    pallas_call x4, Pallas kernels, beams(): pl.pallas_call(functools.partial(beam_kernel, len(covs), NS_STEPS), grid=...  87.4 us
    all_to_all x4, waiting for transfers between devices, send(): lax.all_to_all(spectra, 'blk', split_axis=0, concat_axis=0, tiled=True)  63.5 us
    ppermute x12, starting transfers between devices, exchange(): lax.ppermute(own, 'segment', [(k, k + d) for k in range(segments - d)])  30.8 us
    pallas_call x4, Pallas kernels, doppler(): pl.pallas_call(doppler_kernel, grid=(ranges // rows,), in_specs=[pl.Block...  29 us
    ppermute x12, waiting for transfers between devices, exchange(): lax.ppermute(own, 'segment', [(k, k + d) for k in range(segments - d)])  28.5 us
    all_to_all x4, starting transfers between devices, send(): lax.all_to_all(spectra, 'blk', split_axis=0, concat_axis=0, tiled=True)  20.8 us
    pallas_call x4, Pallas kernels, covariance(): pl.pallas_call(covariance_kernel, grid=(bins // group,), in_specs=[pl.Blo...  7.95 us
  transfers between devices with their start and end apart: 16, of which 3 were waited for; matrix products, arithmetic and copies ran while one was open for 3% of the time, Pallas kernels for 38%

profile of v2, /device:TPU:0, one launch (start us, length us, event | category | flops | bytes accessed | tf_op | source)
XLA Modules:
  0.0 281.8 jit_solution(4691781992285012919)
XLA Ops:
  2.8 7.8 %shard_map.55 = bf16[96,64,256]{2,1,0:T(8,128)(2,1)} custom-call(bf16[64,128,512]{2,1,0:T(8,128)(2,1)} %bitcast.34, bf16[192,512]{1,0:T(8,128)(2,1)} %reshape.167.t_ref), custom_call_target="tpu_custom_call" | custom-call | flops 1610612736 | bytes 11534336 | tf_op jit(solution)/shard_map/pallas_call | solution.py:82
  10.6 6.3 %all-to-all-start.1 = ((bf16[8,12,64,256]{3,2,1,0:T(8,128)(2,1)}), bf16[8,12,64,256]{3,2,1,0:T(8,128)(2,1)S(1)}, u32[]{:S(2)}, u32[]{:S(2)}) async-start(bf16[8,12,64,256]{3,2,1,0:T(8,128)(2,1)} %bitcast.38), calls=%async_computation.1 | async-start | bytes 6291456 | tf_op jit(solution)/shard_map/all_to_all | solution.py:307
  17.7 7.2 %shard_map.56 = bf16[64,64,256]{2,1,0:T(8,128)(2,1)} custom-call(bf16[64,128,512]{2,1,0:T(8,128)(2,1)} %bitcast.35, bf16[128,512]{1,0:T(8,128)(2,1)} %bitcast.44, bf16[8,12,64,256]{3,2,1,0:T(8,128)(2,1)} %bitcast.39), custom_call_target="tpu_custom_call" | custom-call | flops 1073741824 | bytes 10485760 | tf_op jit(solution)/shard_map/pallas_call | solution.py:82
  25.0 63.5 %all-to-all-done.1.y_ref.refs_3_ = bf16[8,12,64,256]{3,2,1,0:T(8,128)(2,1)S(1)} async-done(((bf16[8,12,64,256]{3,2,1,0:T(8,128)(2,1)}), bf16[8,12,64,256]{3,2,1,0:T(8,128)(2,1)S(1)}, u32[]{:S(2)}, u32[]{:S(2)}) %all-to-all-start.1) | async-done | bytes 3145760 | tf_op jit(solution)/shard_map/all_to_all | solution.py:307
  88.5 4.3 %all-to-all-start = ((bf16[8,8,64,256]{3,2,1,0:T(8,128)(2,1)}), bf16[8,8,64,256]{3,2,1,0:T(8,128)(2,1)}, u32[]{:S(2)}, u32[]{:S(2)}) async-start(bf16[8,8,64,256]{3,2,1,0:T(8,128)(2,1)} %bitcast.41), calls=%async_computation | async-start | bytes 4194304 | tf_op jit(solution)/shard_map/all_to_all | solution.py:307
  93.7 2.4 shard_map.58
  96.1 4.4 %collective-permute-start.3 = (f32[12,128,128]{2,1,0:T(8,128)S(1)}, f32[12,128,128]{2,1,0:T(8,128)}, u32[]{:S(2)}, u32[]{:S(2)}) collective-permute-start(f32[12,128,128]{2,1,0:T(8,128)S(1)} %shard_map.58), channel_id=1, source_target_pairs={{0,8},{8,16},{16,24},{1,9},{9,17},{17,25},{2,10},{10,18},{18,26},{... | collective-permute-start | bytes 2359304 | tf_op jit(solution)/shard_map/ppermute | solution.py:315
  100.5 3.4 %collective-permute-start.4 = (f32[12,128,128]{2,1,0:T(8,128)S(1)}, f32[12,128,128]{2,1,0:T(8,128)}, u32[]{:S(2)}, u32[]{:S(2)}) collective-permute-start(f32[12,128,128]{2,1,0:T(8,128)S(1)} %shard_map.58), channel_id=1, source_target_pairs={{0,16},{8,24},{1,17},{9,25},{2,18},{10,26},{3,19},{11,27},{4,20},{... | collective-permute-start | bytes 2359304 | tf_op jit(solution)/shard_map/ppermute | solution.py:315
  103.9 2.2 collective-permute-start.5
  106.1 11.3 %collective-permute-done.3.refs_0_ = f32[12,128,128]{2,1,0:T(8,128)} collective-permute-done((f32[12,128,128]{2,1,0:T(8,128)S(1)}, f32[12,128,128]{2,1,0:T(8,128)}, u32[]{:S(2)}, u32[]{:S(2)}) %collective-permute-start.3) | collective-permute-done | bytes 786464 | tf_op jit(solution)/shard_map/ppermute | solution.py:315
  117.4 17.2 %collective-permute-done.4.refs_1_ = f32[12,128,128]{2,1,0:T(8,128)} collective-permute-done((f32[12,128,128]{2,1,0:T(8,128)S(1)}, f32[12,128,128]{2,1,0:T(8,128)}, u32[]{:S(2)}, u32[]{:S(2)}) %collective-permute-start.4) | collective-permute-done | bytes 786464 | tf_op jit(solution)/shard_map/ppermute | solution.py:315
  134.6 7.3 %shard_map.62 = bf16[64,64,256]{2,1,0:T(8,128)(2,1)} custom-call(bf16[64,128,512]{2,1,0:T(8,128)(2,1)} %bitcast.36, bf16[128,512]{1,0:T(8,128)(2,1)} %bitcast.43, f32[12,128,128]{2,1,0:T(8,128)} %collective-permute-done.3.refs_0_, f32[12,128,128]{2,1,0:T(8,128)} %collective-permute-done.4.refs_1_, f32[12,128,128]{2,1,0:T(8,128)} %collective-permute-done.5.refs_2_), custom_call_target="tpu_custom_call" | custom-call | flops 1073741824 | bytes 10485760 | tf_op jit(solution)/shard_map/pallas_call | solution.py:82
  141.9 4.9 %all-to-all-start.3 = ((bf16[8,8,64,256]{3,2,1,0:T(8,128)(2,1)}), bf16[8,8,64,256]{3,2,1,0:T(8,128)(2,1)}, u32[]{:S(2)}, u32[]{:S(2)}) async-start(bf16[8,8,64,256]{3,2,1,0:T(8,128)(2,1)} %bitcast.40), calls=%async_computation.3 | async-start | bytes 4194304 | tf_op jit(solution)/shard_map/all_to_all | solution.py:307
  146.9 2.6 fusion.2
  153.7 2.3 shard_map.57
  156.0 3.8 %collective-permute-start = (f32[8,128,128]{2,1,0:T(8,128)S(1)}, f32[8,128,128]{2,1,0:T(8,128)S(1)}, u32[]{:S(2)}, u32[]{:S(2)}) collective-permute-start(f32[8,128,128]{2,1,0:T(8,128)S(1)} %shard_map.57), channel_id=1, source_target_pairs={{0,8},{8,16},{16,24},{1,9},{9,17},{17,25},{2,10},{10,18},{18,26},{... | collective-permute-start | bytes 1572872 | tf_op jit(solution)/shard_map/ppermute | solution.py:315
  159.8 5.3 %collective-permute-start.1 = (f32[8,128,128]{2,1,0:T(8,128)S(1)}, f32[8,128,128]{2,1,0:T(8,128)}, u32[]{:S(2)}, u32[]{:S(2)}) collective-permute-start(f32[8,128,128]{2,1,0:T(8,128)S(1)} %shard_map.57), channel_id=1, source_target_pairs={{0,16},{8,24},{1,17},{9,25},{2,18},{10,26},{3,19},{11,27},{4,20},{... | collective-permute-start | bytes 1572872 | tf_op jit(solution)/shard_map/ppermute | solution.py:315
  167.2 32.0 %shard_map.59 = (bf16[1,32,512,256]{3,2,1,0:T(8,128)(2,1)}, f32[8,128]{1,0:T(8,128)S(1)}) custom-call(f32[12,128,128]{2,1,0:T(8,128)} %collective-permute-done.3.refs_0_, f32[12,128,128]{2,1,0:T(8,128)} %collective-permute-done.4.refs_1_, f32[12,128,128]{2,1,0:T(8,128)} %collective-permute-done.5.refs_2_, ...), custom_call_target="tpu_custom_call" | custom-call | flops 14495514624 | bytes 6291456 | tf_op jit(solution)/shard_map/pallas_call | solution.py:241
  200.6 6.7 %shard_map.60 = bf16[32,64,256]{2,1,0:T(8,128)(2,1)} custom-call(bf16[64,128,512]{2,1,0:T(8,128)(2,1)} %bitcast.37, bf16[64,512]{1,0:T(8,128)(2,1)} %reshape.165.t_ref, f32[8,128,128]{2,1,0:T(8,128)} %copy-done, f32[8,128,128]{2,1,0:T(8,128)} %collective-permute-done.1.refs_1_, f32[8,128,128]{2,1,0:T(8,128)} %collective-permute-done.2.refs_2_, ...), custom_call_target="tpu_custom_call" | custom-call | flops 536870912 | bytes 9437184 | tf_op jit(solution)/shard_map/pallas_call | solution.py:82
  207.3 5.2 %all-to-all-start.2 = ((bf16[8,4,64,256]{3,2,1,0:T(8,128)(2,1)}), bf16[8,4,64,256]{3,2,1,0:T(8,128)(2,1)S(1)}, u32[]{:S(2)}, u32[]{:S(2)}) async-start(bf16[8,4,64,256]{3,2,1,0:T(8,128)(2,1)} %bitcast.42), calls=%async_computation.2 | async-start | bytes 2097152 | tf_op jit(solution)/shard_map/all_to_all | solution.py:307
  213.3 2.3 shard_map.63
  221.0 22.3 %shard_map.64 = (bf16[1,32,512,256]{3,2,1,0:T(8,128)(2,1)}, f32[8,128]{1,0:T(8,128)}) custom-call(f32[8,128,128]{2,1,0:T(8,128)S(1)} %copy-done.1, f32[8,128,128]{2,1,0:T(8,128)} %collective-permute-done.1.refs_1_, f32[8,128,128]{2,1,0:T(8,128)} %collective-permute-done.2.refs_2_, ...), custom_call_target="tpu_custom_call", output_to_operand_aliasing={{0}: (7, {})} | custom-call | flops 9663676416 | bytes 4194304 | tf_op jit(solution)/shard_map/pallas_call | solution.py:241
  248.6 22.3 %shard_map.65 = (bf16[1,32,512,256]{3,2,1,0:T(8,128)(2,1)}, f32[8,128]{1,0:T(8,128)}) custom-call(f32[8,128,128]{2,1,0:T(8,128)} %collective-permute-done.9.refs_0_, f32[8,128,128]{2,1,0:T(8,128)S(1)} %collective-permute-done.10.refs_1_, f32[8,128,128]{2,1,0:T(8,128)} %collective-permute-done.11.refs_2_, ...), custom_call_target="tpu_custom_call", output_to_operand_aliasing={{0}: (7, {})} | custom-call | flops 9663676416 | bytes 4194304 | tf_op jit(solution)/shard_map/pallas_call | solution.py:241
  270.9 10.9 %shard_map.66 = (bf16[1,32,512,256]{3,2,1,0:T(8,128)(2,1)}, f32[8,128]{1,0:T(8,128)}) custom-call(f32[4,128,128]{2,1,0:T(8,128)S(1)} %collective-permute-done.6.refs_0_, f32[4,128,128]{2,1,0:T(8,128)S(1)} %collective-permute-done.7.refs_1_, f32[4,128,128]{2,1,0:T(8,128)S(1)} %collective-permute-done.8.refs_2_, ...), custom_call_target="tpu_custom_call", output_to_operand_aliasing={{0}: (7, {})} | custom-call | flops 4831838208 | bytes 2097152 | tf_op jit(solution)/shard_map/pallas_call | solution.py:241
  (66 shorter events, 23.6 us)
Async XLA Ops:
  2.0 14.9 %copy-start.3 = (bf16[1,8,32,256]{3,2,1,0:T(8,128)(2,1)}, bf16[1,8,32,256]{3,2,1,0:T(8,128)(2,1)S(1)}, u32[]{:S(2)}) copy-start(bf16[1,8,32,256]{3,2,1,0:T(8,128)(2,1)S(1)} %get-tuple-element.24) | copy-start | bytes 393220
  10.6 77.9 %all-to-all-start.1 = ((bf16[8,12,64,256]{3,2,1,0:T(8,128)(2,1)}), bf16[8,12,64,256]{3,2,1,0:T(8,128)(2,1)S(1)}, u32[]{:S(2)}, u32[]{:S(2)}) async-start(bf16[8,12,64,256]{3,2,1,0:T(8,128)(2,1)} %bitcast.38), calls=%async_computation.1 | async-start | bytes 6291456 | tf_op jit(solution)/shard_map/all_to_all | solution.py:307
  25.0 67.9 %copy-start.5 = (s32[1,32,6]{1,0,2:T(1,128)S(1)}, s32[1,32,6]{1,0,2:T(1,128)}, u32[]{:S(2)}) copy-start(s32[1,32,6]{1,0,2:T(1,128)} %param.6) | copy-start | bytes 2308
  25.0 67.9 %copy-start.6 = (s32[1,32]{1,0:T(1,128)S(1)}, s32[1,32]{1,0:T(1,128)}, u32[]{:S(2)}) copy-start(s32[1,32]{1,0:T(1,128)} %param.7) | copy-start | bytes 388
  88.5 53.4 %all-to-all-start = ((bf16[8,8,64,256]{3,2,1,0:T(8,128)(2,1)}), bf16[8,8,64,256]{3,2,1,0:T(8,128)(2,1)}, u32[]{:S(2)}, u32[]{:S(2)}) async-start(bf16[8,8,64,256]{3,2,1,0:T(8,128)(2,1)} %bitcast.41), calls=%async_computation | async-start | bytes 4194304 | tf_op jit(solution)/shard_map/all_to_all | solution.py:307
  93.1 0.6 copy-start.4
  96.1 21.3 %collective-permute-start.3 = (f32[12,128,128]{2,1,0:T(8,128)S(1)}, f32[12,128,128]{2,1,0:T(8,128)}, u32[]{:S(2)}, u32[]{:S(2)}) collective-permute-start(f32[12,128,128]{2,1,0:T(8,128)S(1)} %shard_map.58), channel_id=1, source_target_pairs={{0,8},{8,16},{16,24},{1,9},{9,17},{17,25},{2,10},{10,18},{18,26},{... | collective-permute-start | bytes 2359304 | tf_op jit(solution)/shard_map/ppermute | solution.py:315
  100.5 34.1 %collective-permute-start.4 = (f32[12,128,128]{2,1,0:T(8,128)S(1)}, f32[12,128,128]{2,1,0:T(8,128)}, u32[]{:S(2)}, u32[]{:S(2)}) collective-permute-start(f32[12,128,128]{2,1,0:T(8,128)S(1)} %shard_map.58), channel_id=1, source_target_pairs={{0,16},{8,24},{1,17},{9,25},{2,18},{10,26},{3,19},{11,27},{4,20},{... | collective-permute-start | bytes 2359304 | tf_op jit(solution)/shard_map/ppermute | solution.py:315
  103.9 30.7 %collective-permute-start.5 = (f32[12,128,128]{2,1,0:T(8,128)S(1)}, f32[12,128,128]{2,1,0:T(8,128)}, u32[]{:S(2)}, u32[]{:S(2)}) collective-permute-start(f32[12,128,128]{2,1,0:T(8,128)S(1)} %shard_map.58), channel_id=1, source_target_pairs={{0,24},{1,25},{2,26},{3,27},{4,28},{5,29},{6,30},{7,31}} | collective-permute-start | bytes 2359304 | tf_op jit(solution)/shard_map/ppermute | solution.py:315
  141.9 4.9 %copy-start.7 = (f32[64]{0:T(128)S(1)}, f32[64]{0:T(128)}, u32[]{:S(2)}) copy-start(f32[64]{0:T(128)} %param.9) | copy-start | bytes 772
  141.9 65.4 %all-to-all-start.3 = ((bf16[8,8,64,256]{3,2,1,0:T(8,128)(2,1)}), bf16[8,8,64,256]{3,2,1,0:T(8,128)(2,1)}, u32[]{:S(2)}, u32[]{:S(2)}) async-start(bf16[8,8,64,256]{3,2,1,0:T(8,128)(2,1)} %bitcast.40), calls=%async_computation.3 | async-start | bytes 4194304 | tf_op jit(solution)/shard_map/all_to_all | solution.py:307
  156.0 43.8 %collective-permute-start = (f32[8,128,128]{2,1,0:T(8,128)S(1)}, f32[8,128,128]{2,1,0:T(8,128)S(1)}, u32[]{:S(2)}, u32[]{:S(2)}) collective-permute-start(f32[8,128,128]{2,1,0:T(8,128)S(1)} %shard_map.57), channel_id=1, source_target_pairs={{0,8},{8,16},{16,24},{1,9},{9,17},{17,25},{2,10},{10,18},{18,26},{... | collective-permute-start | bytes 1572872 | tf_op jit(solution)/shard_map/ppermute | solution.py:315
  159.8 40.0 %collective-permute-start.1 = (f32[8,128,128]{2,1,0:T(8,128)S(1)}, f32[8,128,128]{2,1,0:T(8,128)}, u32[]{:S(2)}, u32[]{:S(2)}) collective-permute-start(f32[8,128,128]{2,1,0:T(8,128)S(1)} %shard_map.57), channel_id=1, source_target_pairs={{0,16},{8,24},{1,17},{9,25},{2,18},{10,26},{3,19},{11,27},{4,20},{... | collective-permute-start | bytes 1572872 | tf_op jit(solution)/shard_map/ppermute | solution.py:315
  165.1 34.7 %collective-permute-start.2 = (f32[8,128,128]{2,1,0:T(8,128)S(1)}, f32[8,128,128]{2,1,0:T(8,128)}, u32[]{:S(2)}, u32[]{:S(2)}) collective-permute-start(f32[8,128,128]{2,1,0:T(8,128)S(1)} %shard_map.57), channel_id=1, source_target_pairs={{0,24},{1,25},{2,26},{3,27},{4,28},{5,29},{6,30},{7,31}} | collective-permute-start | bytes 1572872 | tf_op jit(solution)/shard_map/ppermute | solution.py:315
  199.2 0.6 copy-start.2
  199.8 0.8 copy-start
  207.3 13.8 %copy-start.1 = (f32[8,128,128]{2,1,0:T(8,128)S(1)}, f32[8,128,128]{2,1,0:T(8,128)}, u32[]{:S(2)}) copy-start(f32[8,128,128]{2,1,0:T(8,128)} %copy-done) | copy-start | bytes 1572868
  207.3 36.0 %all-to-all-start.2 = ((bf16[8,4,64,256]{3,2,1,0:T(8,128)(2,1)}), bf16[8,4,64,256]{3,2,1,0:T(8,128)(2,1)S(1)}, u32[]{:S(2)}, u32[]{:S(2)}) async-start(bf16[8,4,64,256]{3,2,1,0:T(8,128)(2,1)} %bitcast.42), calls=%async_computation.2 | async-start | bytes 2097152 | tf_op jit(solution)/shard_map/all_to_all | solution.py:307
  215.5 31.5 %collective-permute-start.10 = (f32[8,128,128]{2,1,0:T(8,128)S(1)}, f32[8,128,128]{2,1,0:T(8,128)S(1)}, u32[]{:S(2)}, u32[]{:S(2)}) collective-permute-start(f32[8,128,128]{2,1,0:T(8,128)S(1)} %shard_map.63), channel_id=1, source_target_pairs={{0,16},{8,24},{1,17},{9,25},{2,18},{10,26},{3,19},{11,27},{4,20},{... | collective-permute-start | bytes 1572872 | tf_op jit(solution)/shard_map/ppermute | solution.py:315
  216.9 31.7 %collective-permute-start.11 = (f32[8,128,128]{2,1,0:T(8,128)S(1)}, f32[8,128,128]{2,1,0:T(8,128)}, u32[]{:S(2)}, u32[]{:S(2)}) collective-permute-start(f32[8,128,128]{2,1,0:T(8,128)S(1)} %shard_map.63), channel_id=1, source_target_pairs={{0,24},{1,25},{2,26},{3,27},{4,28},{5,29},{6,30},{7,31}} | collective-permute-start | bytes 1572872 | tf_op jit(solution)/shard_map/ppermute | solution.py:315
  219.0 29.6 %collective-permute-start.9 = (f32[8,128,128]{2,1,0:T(8,128)S(1)}, f32[8,128,128]{2,1,0:T(8,128)}, u32[]{:S(2)}, u32[]{:S(2)}) collective-permute-start(f32[8,128,128]{2,1,0:T(8,128)S(1)} %shard_map.63), channel_id=1, source_target_pairs={{0,8},{8,16},{16,24},{1,9},{9,17},{17,25},{2,10},{10,18},{18,26},{... | collective-permute-start | bytes 1572872 | tf_op jit(solution)/shard_map/ppermute | solution.py:315
  244.4 26.5 %collective-permute-start.6 = (f32[4,128,128]{2,1,0:T(8,128)S(1)}, f32[4,128,128]{2,1,0:T(8,128)S(1)}, u32[]{:S(2)}, u32[]{:S(2)}) collective-permute-start(f32[4,128,128]{2,1,0:T(8,128)S(1)} %shard_map.61), channel_id=1, source_target_pairs={{0,8},{8,16},{16,24},{1,9},{9,17},{17,25},{2,10},{10,18},{18,26},{... | collective-permute-start | bytes 786440 | tf_op jit(solution)/shard_map/ppermute | solution.py:315
  245.7 25.2 %collective-permute-start.7 = (f32[4,128,128]{2,1,0:T(8,128)S(1)}, f32[4,128,128]{2,1,0:T(8,128)S(1)}, u32[]{:S(2)}, u32[]{:S(2)}) collective-permute-start(f32[4,128,128]{2,1,0:T(8,128)S(1)} %shard_map.61), channel_id=1, source_target_pairs={{0,16},{8,24},{1,17},{9,25},{2,18},{10,26},{3,19},{11,27},{4,20},{... | collective-permute-start | bytes 786440 | tf_op jit(solution)/shard_map/ppermute | solution.py:315
  247.0 23.9 %collective-permute-start.8 = (f32[4,128,128]{2,1,0:T(8,128)S(1)}, f32[4,128,128]{2,1,0:T(8,128)S(1)}, u32[]{:S(2)}, u32[]{:S(2)}) collective-permute-start(f32[4,128,128]{2,1,0:T(8,128)S(1)} %shard_map.61), channel_id=1, source_target_pairs={{0,24},{1,25},{2,26},{3,27},{4,28},{5,29},{6,30},{7,31}} | collective-permute-start | bytes 786440 | tf_op jit(solution)/shard_map/ppermute | solution.py:315
